TPU v7x, 32 devices: a whole 2x2x4 slice. The times are simulated.
32 devices in a mesh: grp: 4 (over y, x), row: 8 (over z, core).
Axes of the slice: x: 2, y: 2, z: 4, core: 2. Of those that a mesh axis runs over, the one named last changes fastest.
Arguments:
- snapshots: float32 [16, 4, 65536], P('grp', None, 'row'), may hold values from -12 to 12
- basis: float32 [128, 262144], P(None, ('grp', 'row')), may hold values from -4 to 4
- assignment: int32 [16], replicated, may hold values from 0 to 15, each once
- param_index: int32 [16], replicated, may hold values from 0 to 63
- offsets: int32 [8, 262144], P(None, ('grp', 'row')), may hold values from -2048 to 2048, as said below
- coefs: float32 [2, 8, 262144], P(None, None, ('grp', 'row')), may hold values from -2.5 to 2.5
Outputs:
- new_columns: float32 [16, 262144], P(None, ('grp', 'row'))
- applied: float32 [2, 16, 262144], P(None, None, ('grp', 'row'))
- coords: float32 [128, 16], replicated
- r_factor: float32 [16, 16], replicated
- reduced: float32 [2, 144, 16], replicated
- estimate: float32 [16], replicated
Inputs may be any that keep to these rules, and one draw needn't show every extreme that they name: `offsets`: both ends of the range occur in every draw.
All inputs are finite; a program needn't handle non-finite values.
Results may differ from a plain program's by a relative error of at most 0.00029.
Values sent between devices are 32-bit elements; how exact they have to be, the bound alone decides.
A program may use at most 64 MiB of HBM per device.

v0:
```python
import jax
import jax.numpy as jnp
from jax import lax
from jax.sharding import PartitionSpec as P

NPARAM = 64


def extended_2(block, sides, width):
    for axis, dim in sides:
        count = lax.axis_size(axis)
        forward = [(i, i + 1) for i in range(count - 1)]
        backward = [(target, source) for source, target in forward]
        low = lax.ppermute(
            lax.slice_in_dim(block, block.shape[dim] - width, None, axis=dim), axis, forward
        )
        high = lax.ppermute(lax.slice_in_dim(block, 0, width, axis=dim), axis, backward)
        block = jnp.concatenate([low, block, high], axis=dim)
    return block


def cholesky_lower(matrix):
    order = matrix.shape[0]
    index_list = jnp.arange(order, dtype=jnp.int32)

    def cholesky_step(column_index, factor):
        column = lax.dynamic_slice_in_dim(matrix, column_index, 1, 1)[:, 0]
        factor_row = lax.dynamic_slice_in_dim(factor, column_index, 1, 0)[0]
        column = column - jnp.dot(factor, factor_row, precision=lax.Precision.HIGHEST)
        pivot = jnp.sqrt(jnp.sum(jnp.where(index_list == column_index, column, 0.0)))
        fresh = jnp.where(
            index_list > column_index,
            column / pivot,
            jnp.where(index_list == column_index, pivot, 0.0),
        )
        return lax.dynamic_update_slice_in_dim(factor, fresh[:, None], column_index, 1)

    return lax.fori_loop(0, order, cholesky_step, jnp.zeros(matrix.shape, matrix.dtype))


def forward_solve(lower, right):
    order = lower.shape[0]

    def forward_step(row_index, solved):
        lower_row = lax.dynamic_slice_in_dim(lower, row_index, 1, 0)[0]
        pivot = jnp.sum(jnp.where(jnp.arange(order, dtype=jnp.int32) == row_index, lower_row, 0.0))
        target = lax.dynamic_slice_in_dim(right, row_index, 1, 0)[0]
        value = (target - jnp.dot(lower_row, solved, precision=lax.Precision.HIGHEST)) / pivot
        return lax.dynamic_update_slice_in_dim(solved, value[None, :], row_index, 0)

    return lax.fori_loop(0, order, forward_step, jnp.zeros(right.shape, right.dtype))


def backward_solve(lower, right):
    order = lower.shape[0]

    def backward_step(turn, solved):
        row_index = order - 1 - turn
        upper_row = lax.dynamic_slice_in_dim(lower, row_index, 1, 1)[:, 0]
        pivot = jnp.sum(jnp.where(jnp.arange(order, dtype=jnp.int32) == row_index, upper_row, 0.0))
        target = lax.dynamic_slice_in_dim(right, row_index, 1, 0)[0]
        value = (target - jnp.dot(upper_row, solved, precision=lax.Precision.HIGHEST)) / pivot
        return lax.dynamic_update_slice_in_dim(solved, value[None, :], row_index, 0)

    return lax.fori_loop(0, order, backward_step, jnp.zeros(right.shape, right.dtype))


def apply_local(extended, offsets, coefs, width):
    row_count = offsets.shape[1]
    positions = jnp.arange(row_count, dtype=jnp.int32) + width
    totals = [
        jnp.zeros((extended.shape[0], row_count), jnp.float32)
        for term_index in range(coefs.shape[0])
    ]
    for slot_index in range(offsets.shape[0]):
        picked = jnp.take(extended, positions + offsets[slot_index], axis=1)
        totals = [
            totals[term_index] + coefs[term_index, slot_index][None, :] * picked
            for term_index in range(len(totals))
        ]
    return jnp.stack(totals)


def body(snapshots, basis, assignment, param_index, offsets, coefs):
    highest = lax.Precision.HIGHEST
    snap_count = assignment.shape[0]
    local_rows = basis.shape[1]
    total_rows = local_rows * lax.axis_size("grp") * lax.axis_size("row")
    width = local_rows // 4
    received = lax.all_to_all(snapshots, "grp", split_axis=1, concat_axis=0, tiled=True)
    arrived = received.reshape(snap_count, local_rows)
    placing = (assignment[None, :] == jnp.arange(snap_count, dtype=jnp.int32)[:, None]).astype(
        jnp.float32
    )
    ordered = jnp.dot(placing, arrived, precision=highest)
    gram = lax.psum(jnp.dot(basis, basis.T, precision=highest), ("grp", "row")) / total_rows
    basis_lower = cholesky_lower(gram)
    project_sum, snap_sum = lax.psum(
        (
            jnp.dot(basis, ordered.T, precision=highest),
            jnp.dot(ordered, ordered.T, precision=highest),
        ),
        ("grp", "row"),
    )
    project = project_sum / total_rows
    halfway = forward_solve(basis_lower, project)
    coords = backward_solve(basis_lower, halfway)
    residual = ordered - jnp.dot(coords.T, basis, precision=highest)
    cross = jnp.dot(project.T, coords, precision=highest)
    curved = jnp.dot(coords.T, jnp.dot(gram, coords, precision=highest), precision=highest)
    residual_gram = snap_sum / total_rows - cross - cross.T + curved
    residual_gram = 0.5 * (residual_gram + residual_gram.T)
    lower = cholesky_lower(residual_gram)
    inverse = forward_solve(lower, jnp.eye(snap_count, dtype=jnp.float32))
    new_columns = jnp.dot(inverse, residual, precision=highest)
    extended = extended_2(new_columns, ((("grp", "row"), 1),), width)
    applied = apply_local(extended, offsets, coefs, width)
    blocks = []
    for term_index in range(coefs.shape[0]):
        upper_part = jnp.dot(basis, applied[term_index].T, precision=highest)
        lower_part = jnp.dot(new_columns, applied[term_index].T, precision=highest)
        blocks.append(jnp.concatenate([upper_part, lower_part], axis=0))
    viscosity = 0.5 + param_index.astype(jnp.float32) / NPARAM
    combined = applied[0]
    term_index = 1
    combined = combined + (viscosity**term_index)[:, None] * applied[term_index]
    block_sum, square_sum = lax.psum(
        (jnp.stack(blocks), jnp.sum(combined * combined, axis=1)), ("grp", "row")
    )
    reduced = block_sum / total_rows
    estimate = square_sum / total_rows
    return (new_columns, applied, coords, lower.T, reduced, estimate)


def solution(mesh):
    return jax.shard_map(
        body,
        mesh=mesh,
        in_specs=(
            P("grp", None, "row"),
            P(None, ("grp", "row")),
            P(),
            P(),
            P(None, ("grp", "row")),
            P(None, None, ("grp", "row")),
        ),
        out_specs=(P(None, ("grp", "row")), P(None, None, ("grp", "row")), P(), P(), P(), P()),
        check_vma=False,
    )
```

profile of v0, /device:TPU:0, one launch (start us, length us, event | category | flops | bytes accessed | tf_op | source)
XLA Modules:
  0.0 1223.7 jit_solution(2992273450105122434)
XLA Ops:
  9.3 5.2 all-to-all-start
  14.6 7.6 fusion.64
  25.6 116.0 %all-reduce.4.cloned.1.call-done = f32[128,128]{1,0:T(8,128)} async-done(((f32[128,128]{1,0:T(8,128)}), f32[128,128]{1,0:T(8,128)}) %all-reduce.4.cloned.1.call-update) | async-done | bytes 65552 | tf_op jit(solution)/shard_map/psum | solution.py:96
  142.6 258.7 %while.74 = (s32[]{:T(128)}, f32[128,128]{1,0:T(8,128)S(1)}, f32[128,128]{0,1:T(8,128)S(1)}, s32[]{:T(128)}, s32[]{:T(128)}) while((s32[]{:T(128)}, f32[128,128]{1,0:T(8,128)S(1)}, f32[128,128]{0,1:T(8,128)S(1)}, s32[]{:T(128)}, s32[]{:T(128)}) %tuple.200), condition=%wide.region_5.6_spmd.clone.clone, body=%wide.region_3.5_spmd.clone.clone.sunk | while | flops 197761 | bytes 71765 | solution.py:38
  402.0 5.1 convolution_bitcast_fusion.7
  407.9 41.0 %all-reduce.1 = (f32[128,16]{0,1:T(8,128)S(1)}, f32[16,16]{1,0:T(8,128)S(1)}) all-reduce(f32[128,16]{0,1:T(8,128)S(1)} %convolution_bitcast_fusion.7, f32[16,16]{1,0:T(8,128)S(1)} %fusion.63), channel_id=1, replica_groups=mesh['grp'=4,'row'=8] {'grp','row'}, use_global_device_ids=true, to_apply=%region_1.2 | all-reduce | flops 2304 | bytes 18432 | tf_op jit(solution)/shard_map/psum | solution.py:98
  449.0 186.3 %while.71 = (s32[]{:T(128)}, f32[128,16]{1,0:T(8,128)S(1)}, f32[128,16]{1,0:T(8,128)S(1)}, f32[128,128]{1,0:T(8,128)S(1)}, s32[]{:T(128)}, /*index=5*/s32[]{:T(128)}) while((s32[]{:T(128)}, f32[128,16]{1,0:T(8,128)S(1)}, f32[128,16]{1,0:T(8,128)S(1)}, f32[128,128]{1,0:T(8,128)S(1)}, s32[]{:T(128)}, /*index=5*/s32[]{:T(128)}) %tuple.203), condition=%wide.region_8.9_spmd, body=%wide.region_6.8_spmd.sunk | while | flops 24993 | bytes 69901 | solution.py:51
  635.3 187.1 %while.72 = (s32[]{:T(128)}, f32[128,16]{1,0:T(8,128)S(1)}, f32[128,16]{1,0:T(8,128)S(1)}, f32[128,128]{0,1:T(8,128)S(1)}, s32[]{:T(128)}, /*index=5*/s32[]{:T(128)}, s32[]{:T(128)}, s32[]{:T(128)}) while((s32[]{:T(128)}, f32[128,16]{1,0:T(8,128)S(1)}, f32[128,16]{1,0:T(8,128)S(1)}, f32[128,128]{0,1:T(8,128)S(1)}, s32[]{:T(128)}, ...), condition=%wide.region_11.12_spmd, body=%wide.region_9.11_spmd.sunk | while | flops 24997 | bytes 68439 | solution.py:65
  822.6 3.8 convolution_subtract_fusion
  827.2 26.0 %while.75 = (s32[]{:T(128)}, f32[16,16]{1,0:T(8,128)S(1)}, f32[16,16]{0,1:T(8,128)S(1)}, s32[]{:T(128)}, s32[]{:T(128)}) while((s32[]{:T(128)}, f32[16,16]{1,0:T(8,128)S(1)}, f32[16,16]{0,1:T(8,128)S(1)}, s32[]{:T(128)}, s32[]{:T(128)}) %tuple.209), condition=%wide.region_14.15_spmd.clone.clone, body=%wide.region_12.14_spmd.clone.clone.sunk | while | flops 3217 | bytes 11285 | solution.py:38
  853.2 22.8 %while.73 = (s32[]{:T(128)}, f32[16,16]{1,0:T(8,128)S(1)}, f32[16,16]{1,0:T(8,128)S(1)}, f32[16,16]{1,0:T(8,128)S(1)}, s32[]{:T(128)}, /*index=5*/s32[]{:T(128)}) while((s32[]{:T(128)}, f32[16,16]{1,0:T(8,128)S(1)}, f32[16,16]{1,0:T(8,128)S(1)}, f32[16,16]{1,0:T(8,128)S(1)}, s32[]{:T(128)}, /*index=5*/s32[]{:T(128)}) %tuple.212), condition=%wide.region_17.18_spmd, body=%wide.region_15.17_spmd.sunk | while | flops 3153 | bytes 12109 | solution.py:51
  881.4 4.0 copy.81
  885.3 30.5 %gather_fusion = f32[8192,16]{1,0:T(8,128)} fusion(f32[16,12288]{0,1:T(8,128)} %copy.81, s32[8192]{0:T(1024)S(1)} %fusion.44), kind=kCustom, calls=%fused_computation.clone | custom fusion | bytes 1081344 | tf_op jit(solution)/shard_map/jit(_take)/gather | solution.py:76
  918.6 30.5 %gather_fusion.1 = f32[8192,16]{1,0:T(8,128)} fusion(f32[16,12288]{0,1:T(8,128)} %copy.81, s32[8192]{0:T(1024)S(1)} %fusion.45), kind=kCustom, calls=%fused_computation.1.clone | custom fusion | bytes 1081344 | tf_op jit(solution)/shard_map/jit(_take)/gather | solution.py:76
  951.9 30.5 %gather_fusion.2 = f32[8192,16]{1,0:T(8,128)} fusion(f32[16,12288]{0,1:T(8,128)} %copy.81, s32[8192]{0:T(1024)S(1)} %fusion.46), kind=kCustom, calls=%fused_computation.2.clone | custom fusion | bytes 1081344 | tf_op jit(solution)/shard_map/jit(_take)/gather | solution.py:76
  985.1 30.5 %gather_fusion.3 = f32[8192,16]{1,0:T(8,128)} fusion(f32[16,12288]{0,1:T(8,128)} %copy.81, s32[8192]{0:T(1024)S(1)} %fusion.47), kind=kCustom, calls=%fused_computation.3.clone | custom fusion | bytes 1081344 | tf_op jit(solution)/shard_map/jit(_take)/gather | solution.py:76
  1015.6 3.5 copy.88
  1019.1 30.5 %gather_fusion.4 = f32[8192,16]{1,0:T(8,128)} fusion(f32[16,12288]{0,1:T(8,128)} %copy.81, s32[8192]{0:T(1024)S(1)} %fusion.48), kind=kCustom, calls=%fused_computation.4.clone | custom fusion | bytes 1081344 | tf_op jit(solution)/shard_map/jit(_take)/gather | solution.py:76
  1053.1 30.5 %gather_fusion.5 = f32[8192,16]{1,0:T(8,128)} fusion(f32[16,12288]{0,1:T(8,128)} %copy.81, s32[8192]{0:T(1024)S(1)} %fusion.49), kind=kCustom, calls=%fused_computation.5.clone | custom fusion | bytes 1081344 | tf_op jit(solution)/shard_map/jit(_take)/gather | solution.py:76
  1087.0 30.5 %gather_fusion.6 = f32[8192,16]{1,0:T(8,128)} fusion(f32[16,12288]{0,1:T(8,128)} %copy.81, s32[8192]{0:T(1024)S(1)} %fusion.50), kind=kCustom, calls=%fused_computation.6.clone | custom fusion | bytes 1081344 | tf_op jit(solution)/shard_map/jit(_take)/gather | solution.py:76
  1117.5 3.5 copy.94
  1121.0 30.5 %gather_fusion.7 = f32[8192,16]{1,0:T(8,128)} fusion(f32[16,12288]{0,1:T(8,128)} %copy.81, s32[8192]{0:T(1024)S(1)} %fusion.51), kind=kCustom, calls=%fused_computation.7.clone | custom fusion | bytes 1081344 | tf_op jit(solution)/shard_map/jit(_take)/gather | solution.py:76
  1151.5 3.5 copy.96
  1166.9 47.8 %all-reduce = (f32[2,144,16]{1,2,0:T(8,128)S(1)}, f32[16]{0:T(128)S(1)}) all-reduce(f32[2,144,16]{1,2,0:T(8,128)S(1)} %pad_maximum_fusion.2, f32[16]{0:T(128)S(1)} %copy-done.7), channel_id=1, replica_groups=mesh['grp'=4,'row'=8] {'grp','row'}, use_global_device_ids=true, to_apply=%region_18.20 | all-reduce | flops 4624 | bytes 36992 | tf_op jit(solution)/shard_map/psum | solution.py:127
  (1477 shorter events, 614.4 us)
Async XLA Ops:
  9.3 392.1 %all-to-all-start = ((f32[4,4,8192]{2,0,1:T(4,128)}), f32[4,4,8192]{2,0,1:T(4,128)S(1)}, u32[]{:S(2)}, u32[]{:S(2)}) async-start(f32[4,4,8192]{2,0,1:T(4,128)} %copy.74), calls=%async_computation | async-start | bytes 1048576 | tf_op jit(solution)/shard_map/all_to_all | solution.py:90
  14.5 7.7 copy-start.3
  14.5 10.0 copy-start.2
  14.5 127.1 %all-reduce.4.cloned.1.call-start = ((), (), s32[]{:S(2)}) async-start(), calls=%async_computation.1 | async-start | bytes 131072 | tf_op jit(solution)/shard_map/psum | solution.py:96
  22.2 379.4 %copy-start.8 = (s32[16]{0:T(128)S(1)}, s32[16]{0:T(128)}, u32[]{:S(2)}) copy-start(s32[16]{0:T(128)} %param.20) | copy-start | bytes 196
  407.1 419.5 %copy-start.4 = (f32[128,128]{1,0:T(8,128)S(1)}, f32[128,128]{1,0:T(8,128)}, u32[]{:S(2)}) copy-start(f32[128,128]{1,0:T(8,128)} %all-reduce.4.cloned.1.call-done) | copy-start | bytes 196612
  635.3 244.1 %copy-start.9 = (s32[16]{0:T(128)S(1)}, s32[16]{0:T(128)}, u32[]{:S(2)}) copy-start(s32[16]{0:T(128)} %param.21) | copy-start | bytes 196
  876.6 286.1 %copy-start.1 = (f32[16,8192]{1,0:T(8,128)}, f32[16,8192]{1,0:T(8,128)S(1)}, u32[]{:S(2)}) copy-start(f32[16,8192]{1,0:T(8,128)S(1)} %fusion.65) | copy-start | bytes 1572868
  876.6 4.7 collective-permute-start
  877.9 3.4 collective-permute-start.1
  1121.0 34.0 %copy-start.5 = (f32[1,1,8192]{2,1,0:T(1,128)S(1)}, f32[1,1,8192]{2,1,0:T(1,128)}, u32[]{:S(2)}) copy-start(f32[1,1,8192]{2,1,0:T(1,128)} %get-tuple-element.621) | copy-start | bytes 98308
  1121.0 34.0 %copy-start.6 = (f32[1,1,8192]{2,1,0:T(1,128)S(1)}, f32[1,1,8192]{2,1,0:T(1,128)}, u32[]{:S(2)}) copy-start(f32[1,1,8192]{2,1,0:T(1,128)} %get-tuple-element.622) | copy-start | bytes 98308
  1155.0 4.3 copy-start
  1159.3 7.6 copy-start.7
Sparse Core Ops, SparseCore 0:
  22.3 119.2 all-reduce.3
where the time goes:
time: 1230 us; the launch traced here: 1220 us
  matrix products  361 us (29%)
  local copies, waits for them, and re-layouts  350 us (28%)
  other arithmetic  175 us (14%)
  waiting for transfers between devices  116 us (9%)
  loops' own time  110 us (9%)
  blocking collectives  88.8 us (7%)
  between operations  14.4 us (1%)
    gather x16, local copies, waits for them, and re-layouts, apply_local(): picked = jnp.take(extended, positions + offsets[slot_index], axis=1)  270 us
    dot_general x144, matrix products, cholesky_step(): jnp.dot(factor, factor_row, precision=lax.Precision.HIGHEST)  117 us
    psum x1, waiting for transfers between devices, body(): lax.psum(jnp.dot(basis, basis.T, precision=highest), ('grp', 'row'))  116 us
    dot_general x144, matrix products, forward_step(): jnp.dot(lower_row, solved, precision=lax.Precision.HIGHEST)  115 us
    another operation x2, loops' own time, cholesky_lower(): lax.fori_loop(0, order, cholesky_step, jnp.zeros(matrix.shape, matrix.dty...  104 us
    dot_general x128, matrix products, backward_step(): jnp.dot(upper_row, solved, precision=lax.Precision.HIGHEST)  102 us
    reduce_sum x144, other arithmetic, forward_step(): jnp.sum(jnp.where(jnp.arange(order, dtype=jnp.int32) == row_index, lower_...  87.3 us
    reduce_sum x128, other arithmetic, backward_step(): jnp.sum(jnp.where(jnp.arange(order, dtype=jnp.int32) == row_index, upper_...  77.7 us
  transfers between devices with their start and end apart: 4, of which 2 were waited for; matrix products, arithmetic and copies ran while one was open for 15% of the time, Pallas kernels for 0%

commit v1 on v0

--- a/solution.py
+++ b/solution.py
@@ -93,7 +93,10 @@
         jnp.float32
     )
     ordered = jnp.dot(placing, arrived, precision=highest)
-    gram = lax.psum(jnp.dot(basis, basis.T, precision=highest), ("grp", "row")) / total_rows
+    gram = (
+        jnp.sum(lax.all_gather(jnp.dot(basis, basis.T, precision=highest), ("grp", "row")), axis=0)
+        / total_rows
+    )
     basis_lower = cholesky_lower(gram)
     project_sum, snap_sum = lax.psum(
         (

time: 1230 us -> 1120 us (0.911)
  waiting for transfers between devices: 116 us -> 7.6 us
    psum x1 -> x0, waiting for transfers between devices: 116 us -> none  [body(): lax.psum(jnp.dot(basis, basis.T, precision=highest), ('grp', 'row'))]
  transfers between devices with their start and end apart: 4 -> 4, of which waited for: 2 -> 1; matrix products, arithmetic and copies ran while one was open for 15% -> 2% of each run, Pallas kernels for 0% -> 0%
where the time goes in v1:
time: 1120 us
  matrix products  361 us (32%)
  local copies, waits for them, and re-layouts  352 us (31%)
  other arithmetic  176 us (16%)
  loops' own time  110 us (10%)
  blocking collectives  87.6 us (8%)
  between operations  14.4 us (1%)
    gather x16, local copies, waits for them, and re-layouts, apply_local(): picked = jnp.take(extended, positions + offsets[slot_index], axis=1)  271 us
    dot_general x144, matrix products, cholesky_step(): jnp.dot(factor, factor_row, precision=lax.Precision.HIGHEST)  117 us
    dot_general x144, matrix products, forward_step(): jnp.dot(lower_row, solved, precision=lax.Precision.HIGHEST)  115 us
    another operation x2, loops' own time, cholesky_lower(): lax.fori_loop(0, order, cholesky_step, jnp.zeros(matrix.shape, matrix.dty...  104 us
    dot_general x128, matrix products, backward_step(): jnp.dot(upper_row, solved, precision=lax.Precision.HIGHEST)  102 us
    reduce_sum x144, other arithmetic, forward_step(): jnp.sum(jnp.where(jnp.arange(order, dtype=jnp.int32) == row_index, lower_...  87.3 us
    reduce_sum x128, other arithmetic, backward_step(): jnp.sum(jnp.where(jnp.arange(order, dtype=jnp.int32) == row_index, upper_...  77.7 us
    dynamic_update_slice x144, local copies, waits for them, and re-layouts, cholesky_step(): lax.dynamic_update_slice_in_dim(factor, fresh[:, None], column_index, 1)  47.2 us
  transfers between devices with their start and end apart: 4, of which 1 were waited for; matrix products, arithmetic and copies ran while one was open for 2% of the time, Pallas kernels for 0%

profile of v1, /device:TPU:0, one launch (start us, length us, event | category | flops | bytes accessed | tf_op | source)
XLA Modules:
  0.0 1117.1 jit_solution(5591544788895336431)
XLA Ops:
  9.3 5.2 all-to-all-start
  14.6 7.6 fusion.64
  27.0 5.1 convolution_bitcast_fusion.7
  32.1 41.2 %all-reduce.1 = (f32[128,16]{0,1:T(8,128)S(1)}, f32[16,16]{1,0:T(8,128)S(1)}) all-reduce(f32[128,16]{0,1:T(8,128)S(1)} %convolution_bitcast_fusion.7, f32[16,16]{1,0:T(8,128)S(1)} %fusion.63), channel_id=1, replica_groups=mesh['grp'=4,'row'=8] {'grp','row'}, use_global_device_ids=true, to_apply=%region_1.2 | all-reduce | flops 2304 | bytes 18432 | tf_op jit(solution)/shard_map/psum | solution.py:101
  73.4 7.6 all-gather.3.cloned.1.call-done
  82.8 258.7 %while.74 = (s32[]{:T(128)}, f32[128,128]{1,0:T(8,128)S(1)}, f32[128,128]{0,1:T(8,128)S(1)}, s32[]{:T(128)}, s32[]{:T(128)}) while((s32[]{:T(128)}, f32[128,128]{1,0:T(8,128)S(1)}, f32[128,128]{0,1:T(8,128)S(1)}, s32[]{:T(128)}, s32[]{:T(128)}) %tuple.198), condition=%wide.region_5.6_spmd.clone.clone, body=%wide.region_3.5_spmd.clone.clone.sunk | while | flops 197761 | bytes 71765 | solution.py:38
  341.6 186.3 %while.71 = (s32[]{:T(128)}, f32[128,16]{1,0:T(8,128)S(1)}, f32[128,16]{1,0:T(8,128)S(1)}, f32[128,128]{1,0:T(8,128)S(1)}, s32[]{:T(128)}, /*index=5*/s32[]{:T(128)}) while((s32[]{:T(128)}, f32[128,16]{1,0:T(8,128)S(1)}, f32[128,16]{1,0:T(8,128)S(1)}, f32[128,128]{1,0:T(8,128)S(1)}, s32[]{:T(128)}, /*index=5*/s32[]{:T(128)}) %tuple.201), condition=%wide.region_8.9_spmd, body=%wide.region_6.8_spmd.sunk | while | flops 24993 | bytes 69901 | solution.py:51
  528.0 187.1 %while.72 = (s32[]{:T(128)}, f32[128,16]{1,0:T(8,128)S(1)}, f32[128,16]{1,0:T(8,128)S(1)}, f32[128,128]{0,1:T(8,128)S(1)}, s32[]{:T(128)}, /*index=5*/s32[]{:T(128)}, s32[]{:T(128)}, s32[]{:T(128)}) while((s32[]{:T(128)}, f32[128,16]{1,0:T(8,128)S(1)}, f32[128,16]{1,0:T(8,128)S(1)}, f32[128,128]{0,1:T(8,128)S(1)}, s32[]{:T(128)}, ...), condition=%wide.region_11.12_spmd, body=%wide.region_9.11_spmd.sunk | while | flops 24997 | bytes 68439 | solution.py:65
  715.5 3.9 convolution_subtract_fusion
  719.8 26.0 %while.75 = (s32[]{:T(128)}, f32[16,16]{1,0:T(8,128)S(1)}, f32[16,16]{0,1:T(8,128)S(1)}, s32[]{:T(128)}, s32[]{:T(128)}) while((s32[]{:T(128)}, f32[16,16]{1,0:T(8,128)S(1)}, f32[16,16]{0,1:T(8,128)S(1)}, s32[]{:T(128)}, s32[]{:T(128)}) %tuple.207), condition=%wide.region_14.15_spmd.clone.clone, body=%wide.region_12.14_spmd.clone.clone.sunk | while | flops 3217 | bytes 11285 | solution.py:38
  745.8 22.8 %while.73 = (s32[]{:T(128)}, f32[16,16]{1,0:T(8,128)S(1)}, f32[16,16]{1,0:T(8,128)S(1)}, f32[16,16]{1,0:T(8,128)S(1)}, s32[]{:T(128)}, /*index=5*/s32[]{:T(128)}) while((s32[]{:T(128)}, f32[16,16]{1,0:T(8,128)S(1)}, f32[16,16]{1,0:T(8,128)S(1)}, f32[16,16]{1,0:T(8,128)S(1)}, s32[]{:T(128)}, /*index=5*/s32[]{:T(128)}) %tuple.210), condition=%wide.region_17.18_spmd, body=%wide.region_15.17_spmd.sunk | while | flops 3153 | bytes 12109 | solution.py:51
  774.8 3.9 copy.79
  778.8 30.6 %gather_fusion = f32[8192,16]{1,0:T(8,128)} fusion(f32[16,12288]{0,1:T(8,128)} %copy.79, s32[8192]{0:T(1024)S(1)} %fusion.44), kind=kCustom, calls=%fused_computation.clone | custom fusion | bytes 1081344 | tf_op jit(solution)/shard_map/jit(_take)/gather | solution.py:76
  812.2 30.7 %gather_fusion.1 = f32[8192,16]{1,0:T(8,128)} fusion(f32[16,12288]{0,1:T(8,128)} %copy.79, s32[8192]{0:T(1024)S(1)} %fusion.45), kind=kCustom, calls=%fused_computation.1.clone | custom fusion | bytes 1081344 | tf_op jit(solution)/shard_map/jit(_take)/gather | solution.py:76
  845.6 30.7 %gather_fusion.2 = f32[8192,16]{1,0:T(8,128)} fusion(f32[16,12288]{0,1:T(8,128)} %copy.79, s32[8192]{0:T(1024)S(1)} %fusion.46), kind=kCustom, calls=%fused_computation.2.clone | custom fusion | bytes 1081344 | tf_op jit(solution)/shard_map/jit(_take)/gather | solution.py:76
  879.1 30.7 %gather_fusion.3 = f32[8192,16]{1,0:T(8,128)} fusion(f32[16,12288]{0,1:T(8,128)} %copy.79, s32[8192]{0:T(1024)S(1)} %fusion.47), kind=kCustom, calls=%fused_computation.3.clone | custom fusion | bytes 1081344 | tf_op jit(solution)/shard_map/jit(_take)/gather | solution.py:76
  909.7 3.5 copy.86
  913.2 30.6 %gather_fusion.4 = f32[8192,16]{1,0:T(8,128)} fusion(f32[16,12288]{0,1:T(8,128)} %copy.79, s32[8192]{0:T(1024)S(1)} %fusion.48), kind=kCustom, calls=%fused_computation.4.clone | custom fusion | bytes 1081344 | tf_op jit(solution)/shard_map/jit(_take)/gather | solution.py:76
  947.4 30.6 %gather_fusion.5 = f32[8192,16]{1,0:T(8,128)} fusion(f32[16,12288]{0,1:T(8,128)} %copy.79, s32[8192]{0:T(1024)S(1)} %fusion.49), kind=kCustom, calls=%fused_computation.5.clone | custom fusion | bytes 1081344 | tf_op jit(solution)/shard_map/jit(_take)/gather | solution.py:76
  981.5 30.6 %gather_fusion.6 = f32[8192,16]{1,0:T(8,128)} fusion(f32[16,12288]{0,1:T(8,128)} %copy.79, s32[8192]{0:T(1024)S(1)} %fusion.50), kind=kCustom, calls=%fused_computation.6.clone | custom fusion | bytes 1081344 | tf_op jit(solution)/shard_map/jit(_take)/gather | solution.py:76
  1012.1 3.5 copy.92
  1015.6 30.6 %gather_fusion.7 = f32[8192,16]{1,0:T(8,128)} fusion(f32[16,12288]{0,1:T(8,128)} %copy.79, s32[8192]{0:T(1024)S(1)} %fusion.51), kind=kCustom, calls=%fused_computation.7.clone | custom fusion | bytes 1081344 | tf_op jit(solution)/shard_map/jit(_take)/gather | solution.py:76
  1046.3 3.5 copy.94
  1061.7 46.4 %all-reduce = (f32[2,144,16]{1,2,0:T(8,128)S(1)}, f32[16]{0:T(128)S(1)}) all-reduce(f32[2,144,16]{1,2,0:T(8,128)S(1)} %pad_maximum_fusion.2, f32[16]{0:T(128)S(1)} %copy-done.6), channel_id=1, replica_groups=mesh['grp'=4,'row'=8] {'grp','row'}, use_global_device_ids=true, to_apply=%region_18.20 | all-reduce | flops 4624 | bytes 36992 | tf_op jit(solution)/shard_map/psum | solution.py:130
  (1476 shorter events, 616.0 us)
Async XLA Ops:
  9.3 16.3 %all-to-all-start = ((f32[4,4,8192]{2,0,1:T(4,128)}), f32[4,4,8192]{2,0,1:T(4,128)S(1)}, u32[]{:S(2)}, u32[]{:S(2)}) async-start(f32[4,4,8192]{2,0,1:T(4,128)} %copy.72), calls=%async_computation | async-start | bytes 1048576 | tf_op jit(solution)/shard_map/all_to_all | solution.py:90
  14.5 7.7 copy-start.3
  14.5 9.4 copy-start.2
  14.5 11.3 %copy-start.7 = (s32[16]{0:T(128)S(1)}, s32[16]{0:T(128)}, u32[]{:S(2)}) copy-start(s32[16]{0:T(128)} %param.20) | copy-start | bytes 196
  14.5 66.5 %all-gather.3.cloned.1.call-start = ((), (), s32[]{:S(2)}) async-start(), calls=%async_computation.1 | async-start | bytes 2162688 | tf_op jit(solution)/shard_map/all_gather | solution.py:97
  527.9 244.9 %copy-start.8 = (s32[16]{0:T(128)S(1)}, s32[16]{0:T(128)}, u32[]{:S(2)}) copy-start(s32[16]{0:T(128)} %param.21) | copy-start | bytes 196
  769.2 288.2 %copy-start.1 = (f32[16,8192]{1,0:T(8,128)}, f32[16,8192]{1,0:T(8,128)S(1)}, u32[]{:S(2)}) copy-start(f32[16,8192]{1,0:T(8,128)S(1)} %fusion.65) | copy-start | bytes 1572868
  769.2 5.5 collective-permute-start
  771.4 3.3 collective-permute-start.1
  1015.6 34.2 %copy-start.4 = (f32[1,1,8192]{2,1,0:T(1,128)S(1)}, f32[1,1,8192]{2,1,0:T(1,128)}, u32[]{:S(2)}) copy-start(f32[1,1,8192]{2,1,0:T(1,128)} %get-tuple-element.615) | copy-start | bytes 98308
  1015.6 34.2 %copy-start.5 = (f32[1,1,8192]{2,1,0:T(1,128)S(1)}, f32[1,1,8192]{2,1,0:T(1,128)}, u32[]{:S(2)}) copy-start(f32[1,1,8192]{2,1,0:T(1,128)} %get-tuple-element.616) | copy-start | bytes 98308
  1049.8 4.3 copy-start
  1054.1 7.6 copy-start.6
Sparse Core Ops, SparseCore 0:
  22.3 58.5 all-gather.2
